TPU v7x, 32 devices: a whole 2x2x4 slice. The times are simulated.
32 devices in a mesh: lon: 8 (over y, x, core), lat: 4 (over z).
Axes of the slice: x: 2, y: 2, z: 4, core: 2. Of those that a mesh axis runs over, the one named last changes fastest.
Arguments:
- height: float32 [768, 7200], P('lat', 'lon'), may hold values from 0.4 to 1.6
- east_wind: float32 [768, 7200], P('lat', 'lon'), may hold values from -1.5 to 1.5
- north_wind: float32 [768, 7200], P('lat', 'lon'), may hold values from -1.5 to 1.5
- cutoffs: int32 [512], replicated, may hold values from 1 to 64
Outputs:
- height_final: float32 [768, 7200], P('lat', 'lon')
- east_final: float32 [768, 7200], P('lat', 'lon')
- north_final: float32 [768, 7200], P('lat', 'lon')
All inputs are finite; a program needn't handle non-finite values.
Results may differ from a plain program's by a relative error of at most 0.0002.
Values sent between devices are 32-bit elements; how exact they have to be, the bound alone decides.
A program may use at most 128 MiB of HBM per device.

v0:
```python
import functools
import math

import jax
import jax.numpy as jnp
import numpy as np
from jax import lax
from jax.experimental import pallas as pl
from jax.experimental.pallas import tpu as pltpu
from jax.sharding import PartitionSpec as P

NLON = 7200
LAT_ROWS = 3600
KMAX = 64
STEPS = 2
COURANT = 0.1
OMEGA_RATE = 1.5

LAT_STEP = math.pi / LAT_ROWS
LON_STEP = 2.0 * math.pi / NLON
TIME_STEP = COURANT * LAT_STEP
COEFFS = 2 * KMAX + 1
TOP = 16
HALO = 4
LANES = 128
MESH = pl.DeviceIdType.MESH


def up_to(value, multiple):
    return -(-value // multiple) * multiple


class Plan:
    def __init__(self, lons, lats, rows, width, filtered):
        self.lons, self.lats, self.rows, self.width = lons, lats, rows, width
        self.filtered = filtered
        self.lanes = up_to(width + 2 * HALO, LANES)
        self.tall = rows + 2 * TOP
        self.part = rows + TOP
        self.cols = up_to(3 * self.part, LANES)
        self.share = up_to(COEFFS, lons) // lons
        self.pad = up_to(self.share, 8)
        self.waves = lons * self.pad


def wave_tables(plan):
    index = np.arange(plan.lons)[:, None] * plan.share + np.arange(plan.pad)[None, :]
    real = (np.arange(plan.pad)[None, :] < plan.share) & (index < COEFFS)
    index = np.where(real, index, 0).reshape(-1)
    wave = np.where(index <= KMAX, index, index - KMAX)
    lane = np.arange(plan.lanes)
    local = np.where(lane < plan.lanes - HALO, lane, lane - plan.lanes)
    column = np.arange(plan.lons)[:, None] * plan.width + local[None, :]
    turn = (wave[None, :, None] * column[:, None, :]) % NLON * (2.0 * math.pi / NLON)
    table = np.where((index <= KMAX)[None, :, None], np.cos(turn), np.sin(turn))
    table = np.where(real.reshape(-1)[None, :, None], table, 0.0).astype(np.float32)
    high = table.astype(jnp.bfloat16)
    low = (table - high.astype(np.float32)).astype(jnp.bfloat16)
    return np.stack([high, low], axis=1)


def row_tables(plan):
    row = np.arange(plan.lats)[:, None] * plan.rows + np.arange(plan.tall)[None, :] - TOP
    angle = (row + 0.5) * LAT_STEP
    cos = np.abs(np.sin(angle))
    north = np.abs(np.sin(angle - LAT_STEP))
    south = np.abs(np.sin(angle + LAT_STEP))
    signed = np.where(row < 0, -1.0, 1.0) / cos
    sin = np.cos(angle)
    half = 0.5 / LAT_STEP
    out = np.stack(
        [0.5 / LON_STEP * signed, half * north / cos, half * south / cos, 2.0 * OMEGA_RATE * sin, sin * signed],
        axis=1,
    )
    return np.broadcast_to(out[..., None], out.shape + (LANES,)).astype(np.float32)


def stage(plan, geo, source, base, target, factor):
    spread = plan.lanes // LANES
    half = 0.5 / LAT_STEP

    @pl.loop(1, plan.tall // 8 - 1)
    def _(tile):
        start = pl.multiple_of(tile * 8, 8)
        here = pl.ds(start, 8)
        around = pl.ds(start - 8, 24)
        a, gn, gs, m3, q = (
            jnp.concatenate([geo[g, here, :]] * spread, axis=1) for g in range(5)
        )
        tiles = [source[f, around, :] for f in range(3)]
        h, u, v = (tile[8:16] for tile in tiles)
        hn, un, vn = (tile[7:15] for tile in tiles)
        hs, us, vs = (tile[9:17] for tile in tiles)

        def zonal(value):
            return pltpu.roll(value, plan.lanes - 1, 1) - pltpu.roll(value, 1, 1)

        ua = u * a
        vb = v * half
        m = m3 + u * q
        fh = -(zonal(h * u) * a) - (hn * vn * gn - hs * vs * gs)
        fu = m * v - ua * zonal(u) - vb * (un - us) - zonal(h) * a
        fv = -(m * u) - ua * zonal(v) - vb * (vn - vs) - half * (hn - hs)
        target[0, here, :] = base[0, here, :] + factor * fh
        target[1, here, :] = base[1, here, :] + factor * fu
        target[2, here, :] = base[2, here, :] + factor * fv


def split(value):
    high = value.astype(jnp.bfloat16)
    return high, (value - high.astype(jnp.float32)).astype(jnp.bfloat16)


def kernel(
    plan, h_in, u_in, v_in, cut_ref, waves_hbm, rows_hbm, h_out, u_out, v_out,
    state, middle, strips, north_strips, got_strips, lines, got_lines,
    waves, geo, work, parts, got_parts, whole, coeffs,
    local_sem, strip_send, strip_recv, line_send, line_recv,
    scatter_send, scatter_recv, gather_send, gather_recv,
):
    lon = lax.axis_index("lon")
    lat = lax.axis_index("lat")
    lons, lats, rows, width, lanes = plan.lons, plan.lats, plan.rows, plan.width, plan.lanes
    tall, part, half = plan.tall, plan.part, plan.lons // 2
    last = lats - 1
    end = TOP + rows
    edge = lanes - LANES
    off = width - edge

    get_waves = pltpu.make_async_copy(waves_hbm.at[lon], waves, local_sem.at[0])
    get_rows = pltpu.make_async_copy(rows_hbm.at[lat], geo, local_sem.at[1])
    get_waves.start()
    get_rows.start()

    def around(by):
        return lax.rem(lon + by + lons, lons)

    barrier = pltpu.get_barrier_semaphore()
    for by in range(1, lons):
        pl.semaphore_signal(barrier, inc=1, device_id={"lon": around(by), "lat": lat}, device_id_type=MESH)

    @pl.when(lat > 0)
    def _():
        for by in (-1, 0, 1):
            pl.semaphore_signal(barrier, inc=1, device_id={"lon": around(by), "lat": lat - 1}, device_id_type=MESH)

    @pl.when(lat < last)
    def _():
        for by in (-1, 0, 1):
            pl.semaphore_signal(barrier, inc=1, device_id={"lon": around(by), "lat": lat + 1}, device_id_type=MESH)

    for f, ref in enumerate((h_in, u_in, v_in)):
        state[f, :TOP, :] = jnp.zeros((TOP, lanes), jnp.float32)
        state[f, end:, :] = jnp.zeros((TOP, lanes), jnp.float32)
        middle[f, :8, :] = jnp.zeros((8, lanes), jnp.float32)
        middle[f, tall - 8 :, :] = jnp.zeros((8, lanes), jnp.float32)
        state[f, TOP:end, edge:] = jnp.zeros((rows, LANES), jnp.float32)
        state[f, TOP:end, :width] = ref[...]
    if plan.cols > 3 * part:
        work[:, 3 * part :, :] = jnp.zeros((2, plan.cols - 3 * part, lanes), jnp.bfloat16)

    blank = jnp.zeros((256 - rows, LANES), jnp.float32)
    for f in range(3):
        at = slice(HALO * f, HALO * f + HALO)
        first = jnp.concatenate([state[f, TOP:end, :LANES], blank], axis=0).T
        final = jnp.concatenate([state[f, TOP:end, edge:], blank], axis=0).T
        strips[0, at, :] = first[:HALO]
        strips[1, at, :] = final[off - HALO : off]
        lines[0, at, :] = state[f, TOP : TOP + HALO, :]
        lines[1, at, :] = state[f, end - HALO : end, :]
    strips[:, 12:, :] = jnp.zeros((2, 4, 256), jnp.float32)
    lines[:, 12:, :] = jnp.zeros((2, 4, lanes), jnp.float32)
    north_strips[...] = strips[...]

    @pl.when(lat == 0)
    def _():
        lane = lax.broadcasted_iota(jnp.int32, (16, 256), 1)
        row = lax.broadcasted_iota(jnp.int32, (16, 256), 0)
        flip = jnp.where(row < HALO, 1.0, -1.0)
        for side in range(2):
            strip = strips[side] * flip
            mirrored = jnp.zeros((16, 256), jnp.float32)
            for i in range(HALO):
                mirrored = jnp.where(lane == rows - 1 - i, strip[:, i : i + 1], mirrored)
            north_strips[side] = mirrored
        for f in range(3):
            sign = 1.0 if f == 0 else -1.0
            for i in range(HALO):
                lines[0, HALO * f + HALO - 1 - i, :] = sign * state[f, TOP + i, :]

    @pl.when(lat == last)
    def _():
        got_strips[:, 2] = jnp.zeros((2, 16, 256), jnp.float32)
        got_lines[1] = jnp.zeros((16, lanes), jnp.float32)

    inner = jnp.logical_and(lat > 0, lat < last)
    pl.semaphore_wait(barrier, jnp.where(inner, lons + 5, lons + 2))

    def strip_copy(source, side, slot, to_lon, to_lat, number):
        return pltpu.make_async_remote_copy(
            src_ref=source.at[side], dst_ref=got_strips.at[1 - side, slot],
            send_sem=strip_send.at[number, side], recv_sem=strip_recv.at[1 - side, slot],
            device_id={"lon": to_lon, "lat": to_lat}, device_id_type=MESH,
        )

    def line_copy(which, slot, to_lon, to_lat):
        return pltpu.make_async_remote_copy(
            src_ref=lines.at[which], dst_ref=got_lines.at[slot],
            send_sem=line_send.at[which], recv_sem=line_recv.at[slot],
            device_id={"lon": to_lon, "lat": to_lat}, device_id_type=MESH,
        )

    at_pole = lat == 0
    turn = jnp.where(at_pole, half, 0)
    to_north = jnp.where(at_pole, 0, lat - 1)
    north_line = line_copy(0, jnp.where(at_pole, 0, 1), around(turn), to_north)
    south_line = line_copy(1, 0, lon, lat + 1)
    north_slot = jnp.where(at_pole, 0, 2)
    north = [
        strip_copy(north_strips, 0, north_slot, around(turn - 1), to_north, 0),
        strip_copy(north_strips, 1, north_slot, around(turn + 1), to_north, 0),
    ]
    level = [strip_copy(strips, 0, 1, around(-1), lat, 1), strip_copy(strips, 1, 1, around(1), lat, 1)]
    south = [strip_copy(strips, 0, 0, around(-1), lat + 1, 2), strip_copy(strips, 1, 0, around(1), lat + 1, 2)]
    north_line.start()

    @pl.when(lat < last)
    def _():
        south_line.start()
        for copy in south:
            copy.start()

    for copy in level + north:
        copy.start()

    for copy in level:
        copy.wait()
    for copy in [north_line] + north:
        copy.wait_send()
    for side in range(2):
        strip_copy(strips, 1 - side, 0, lon, lat, 2).wait_recv()
    line_copy(1, 0, lon, lat).wait_recv()

    @pl.when(lat < last)
    def _():
        south_line.wait_send()
        for copy in south:
            copy.wait_send()
        for side in range(2):
            strip_copy(strips, 1 - side, 2, lon, lat, 2).wait_recv()
        line_copy(1, 1, lon, lat).wait_recv()

    lane = lax.broadcasted_iota(jnp.int32, (16, 256), 1)
    sides = []
    for side in (1, 0):
        sides.append(
            jnp.where(
                lane < TOP,
                pltpu.roll(got_strips[side, 0], (TOP - rows) % 256, 1),
                jnp.where(lane < end, pltpu.roll(got_strips[side, 1], TOP, 1), pltpu.roll(got_strips[side, 2], end, 1)),
            )
        )
    sides.append(jnp.zeros((LANES - 32, 256), jnp.float32))
    halo = jnp.concatenate(sides, axis=0).T[:tall]
    lane = lax.broadcasted_iota(jnp.int32, (tall, LANES), 1)
    for f in range(3):
        state[f, TOP - HALO : TOP, :] = got_lines[0, HALO * f : HALO * f + HALO, :]
        state[f, end : end + HALO, :] = got_lines[1, HALO * f : HALO * f + HALO, :]
        east = pltpu.roll(halo, (off - HALO * f) % LANES, 1)
        west = pltpu.roll(halo, (LANES - HALO - 16 - HALO * f) % LANES, 1)
        state[f, :, edge:] = jnp.where(
            lane >= LANES - HALO,
            west,
            jnp.where((lane >= off) & (lane < off + HALO), east, state[f, :, edge:]),
        )

    def south_rim(ref):
        @pl.when(lat == last)
        def _():
            for f in range(3):
                ref[f, end : end + 1, :] = ref[f, end - 1 : end, :]

    south_rim(state)
    get_rows.wait()
    get_waves.wait()

    for step in range(STEPS):
        stage(plan, geo, state, state, middle, 0.5 * TIME_STEP)
        south_rim(middle)
        stage(plan, geo, middle, state, state, TIME_STEP)

        @pl.loop(0, part // 16)
        def _(tile):
            lane = lax.broadcasted_iota(jnp.int32, (16, lanes), 1)
            start = pl.multiple_of(tile * 16, 16)
            for f in range(3):
                value = jnp.where(lane < width, state[f, pl.ds(start + 8, 16), :], 0.0)
                high, low = split(value)
                work[0, pl.ds(f * part + start, 16), :] = high
                work[1, pl.ds(f * part + start, 16), :] = low

        def against(table, value):
            return lax.dot_general(table, value, (((1,), (1,)), ((), ())), preferred_element_type=jnp.float32)

        for begin in range(0, plan.cols, 256):
            size = min(256, plan.cols - begin)
            high = work[0, begin : begin + size, :]
            low = work[1, begin : begin + size, :]
            total = against(waves[0], high) + (against(waves[0], low) + against(waves[1], high))
            parts[step, :, :, begin : begin + size] = total.reshape(lons, plan.pad, size)

        def scatter(by):
            return pltpu.make_async_remote_copy(
                src_ref=parts.at[step, around(by)], dst_ref=got_parts.at[step, by],
                send_sem=scatter_send.at[step, by], recv_sem=scatter_recv.at[step, by],
                device_id={"lon": around(by), "lat": lat}, device_id_type=MESH,
            )

        def gather(by):
            return pltpu.make_async_remote_copy(
                src_ref=whole.at[step, lon], dst_ref=whole.at[step, lon],
                send_sem=gather_send.at[step, by], recv_sem=gather_recv.at[step, by],
                device_id={"lon": around(by), "lat": lat}, device_id_type=MESH,
            )

        def arriving(by):
            return pltpu.make_async_remote_copy(
                src_ref=whole.at[step, lon], dst_ref=whole.at[step, around(-by)],
                send_sem=gather_send.at[step, by], recv_sem=gather_recv.at[step, by],
                device_id={"lon": around(by), "lat": lat}, device_id_type=MESH,
            )

        for by in range(1, lons):
            scatter(by).start()

        count = plan.filtered
        first_row = lat * rows - 8
        window = pltpu.roll(cut_ref[...], lax.rem(lats * count - first_row, count), 1)[:, :part]
        place = lax.broadcasted_iota(jnp.int32, (1, part), 1)
        for i in range(8):
            window = jnp.where(at_pole & (place == 7 - i), cut_ref[0:1, i : i + 1], window)
        cut = jnp.concatenate([window] * 3 + [jnp.zeros((1, plan.cols - 3 * part), jnp.int32)], axis=1)
        index = lon * plan.share + lax.broadcasted_iota(jnp.int32, (plan.pad, plan.cols), 0)
        wave = jnp.where(index <= KMAX, index, index - KMAX)
        scale = jnp.where(index == 0, 1.0 / NLON, 2.0 / NLON)
        weight = jnp.where(wave <= cut, scale, 0.0)

        total = parts[step, lon]
        for by in range(1, lons):
            scatter(by).wait()
            total = total + got_parts[step, by]
        whole[step, lon] = total * weight
        for by in range(1, lons):
            gather(by).start()
        for by in range(1, lons):
            gather(by).wait_send()
            arriving(by).wait_recv()

        high, low = split(whole[step].reshape(plan.waves, plan.cols).T)
        coeffs[0] = high
        coeffs[1] = low
        limit = count - first_row

        @pl.loop(0, lanes // 256)
        def _(chunk):
            at = pl.ds(pl.multiple_of(chunk * 256, 256), 256)
            thigh = waves[0, :, at]
            tlow = waves[1, :, at]
            row = lax.broadcasted_iota(jnp.int32, (part, 256), 0)
            for f in range(3):
                chigh = coeffs[0, f * part : (f + 1) * part, :]
                clow = coeffs[1, f * part : (f + 1) * part, :]
                value = jnp.dot(chigh, thigh, preferred_element_type=jnp.float32) + (
                    jnp.dot(chigh, tlow, preferred_element_type=jnp.float32)
                    + jnp.dot(clow, thigh, preferred_element_type=jnp.float32)
                )
                state[f, 8 : 8 + part, at] = jnp.where(row < limit, value, state[f, 8 : 8 + part, at])

        if step < STEPS - 1:
            south_rim(state)

    for f, ref in enumerate((h_out, u_out, v_out)):
        ref[...] = state[f, TOP:end, :width]


def shards(plan, height, east_wind, north_wind, cutoffs):
    f32, bf16 = jnp.float32, jnp.bfloat16
    vmem = pl.BlockSpec(memory_space=pltpu.VMEM)
    hbm = pl.BlockSpec(memory_space=pl.ANY)
    lons, tall, lanes = plan.lons, plan.tall, plan.lanes
    dma = pltpu.SemaphoreType.DMA
    block = (STEPS, lons, plan.pad, plan.cols)
    return pl.pallas_call(
        functools.partial(kernel, plan),
        out_shape=[jax.ShapeDtypeStruct(height.shape, f32)] * 3,
        in_specs=[vmem] * 4 + [hbm] * 2,
        out_specs=[vmem] * 3,
        scratch_shapes=[
            pltpu.VMEM((3, tall, lanes), f32),
            pltpu.VMEM((3, tall, lanes), f32),
            pltpu.VMEM((2, 16, 256), f32),
            pltpu.VMEM((2, 16, 256), f32),
            pltpu.VMEM((2, 3, 16, 256), f32),
            pltpu.VMEM((2, 16, lanes), f32),
            pltpu.VMEM((2, 16, lanes), f32),
            pltpu.VMEM((2, plan.waves, lanes), bf16),
            pltpu.VMEM((5, tall, LANES), f32),
            pltpu.VMEM((2, plan.cols, lanes), bf16),
            pltpu.VMEM(block, f32),
            pltpu.VMEM(block, f32),
            pltpu.VMEM(block, f32),
            pltpu.VMEM((2, plan.cols, plan.waves), bf16),
            dma((2,)),
            dma((3, 2)),
            dma((2, 3)),
            dma((2,)),
            dma((2,)),
            dma((STEPS, lons)),
            dma((STEPS, lons)),
            dma((STEPS, lons)),
            dma((STEPS, lons)),
        ],
        compiler_params=pltpu.CompilerParams(
            collective_id=0, has_side_effects=True, vmem_limit_bytes=48 * 1024 * 1024
        ),
    )(
        height, east_wind, north_wind, cutoffs.reshape(1, -1),
        jnp.asarray(wave_tables(plan)), jnp.asarray(row_tables(plan)),
    )


def solution(mesh):
    placed = (P("lat", "lon"), P("lat", "lon"), P("lat", "lon"), P())

    def program(height, east_wind, north_wind, cutoffs):
        lons, lats = mesh.shape["lon"], mesh.shape["lat"]
        rows, width = height.shape[0] // lats, height.shape[1] // lons
        plan = Plan(lons, lats, rows, width, cutoffs.shape[0])
        return jax.shard_map(
            lambda *blocks: tuple(shards(plan, *blocks)),
            mesh=mesh,
            in_specs=placed,
            out_specs=(P("lat", "lon"), P("lat", "lon"), P("lat", "lon")),
            check_vma=False,
        )(height, east_wind, north_wind, cutoffs)

    return program
```

profile of v0, /device:TPU:0, one launch (start us, length us, event | category | flops | bytes accessed | tf_op | source)
XLA Modules:
  0.0 67.5 jit_solution(7886825239028659018)
XLA Ops:
  0.6 0.0 copy-start
  0.6 1.1 %copy-done = f32[192,900]{1,0:T(8,128)S(1)} copy-done((f32[192,900]{1,0:T(8,128)S(1)}, f32[192,900]{1,0:T(8,128)}, u32[]{:S(2)}) %copy-start) | copy-done | bytes 691224
  1.8 0.0 copy-start.1
  1.8 1.1 %copy-done.1 = f32[192,900]{1,0:T(8,128)S(1)} copy-done((f32[192,900]{1,0:T(8,128)S(1)}, f32[192,900]{1,0:T(8,128)}, u32[]{:S(2)}) %copy-start.1) | copy-done | bytes 691224
  2.9 0.0 copy-start.2
  2.9 1.1 %copy-done.2 = f32[192,900]{1,0:T(8,128)S(1)} copy-done((f32[192,900]{1,0:T(8,128)S(1)}, f32[192,900]{1,0:T(8,128)}, u32[]{:S(2)}) %copy-start.2) | copy-done | bytes 691224
  4.0 0.0 copy-start.3
  4.0 0.7 %copy-done.3 = s32[512]{0:T(512)S(1)} copy-done((s32[512]{0:T(512)S(1)}, s32[512]{0:T(512)}, u32[]{:S(2)}) %copy-start.3) | copy-done | bytes 2072
  4.7 60.1 %shard_map.85 = (f32[192,900]{1,0:T(8,128)S(1)}, f32[192,900]{1,0:T(8,128)S(1)}, f32[192,900]{1,0:T(8,128)S(1)}) custom-call(f32[192,900]{1,0:T(8,128)S(1)} %copy-done, f32[192,900]{1,0:T(8,128)S(1)} %copy-done.1, f32[192,900]{1,0:T(8,128)S(1)} %copy-done.2, s32[1,512]{1,0:T(1,128)S(1)} %bitcast.1, bf16[8,2,192,1024]{3,2,1,0:T(8,128)(2,1)} %constant.4.clone.waves_hbm, ...), custom_call_target="tpu_custom_call" | custom-call | tf_op jit(solution)/shard_map/pallas_call | solution.py:393
  64.8 0.9 %copy.12 = f32[192,900]{1,0:T(8,128)} copy(f32[192,900]{1,0:T(8,128)S(1)} %get-tuple-element.6) | data formatting | bytes 1382400
  65.7 0.9 %copy.13 = f32[192,900]{1,0:T(8,128)} copy(f32[192,900]{1,0:T(8,128)S(1)} %get-tuple-element.7) | data formatting | bytes 1382400
  66.6 0.9 %copy.14 = f32[192,900]{1,0:T(8,128)} copy(f32[192,900]{1,0:T(8,128)S(1)} %get-tuple-element.8) | data formatting | bytes 1382400
Async XLA Ops:
  0.6 1.1 %copy-start = (f32[192,900]{1,0:T(8,128)S(1)}, f32[192,900]{1,0:T(8,128)}, u32[]{:S(2)}) copy-start(f32[192,900]{1,0:T(8,128)} %h_in.1) | copy-start | bytes 2073604
  1.8 1.1 %copy-start.1 = (f32[192,900]{1,0:T(8,128)S(1)}, f32[192,900]{1,0:T(8,128)}, u32[]{:S(2)}) copy-start(f32[192,900]{1,0:T(8,128)} %u_in.1) | copy-start | bytes 2073604
  2.9 1.1 %copy-start.2 = (f32[192,900]{1,0:T(8,128)S(1)}, f32[192,900]{1,0:T(8,128)}, u32[]{:S(2)}) copy-start(f32[192,900]{1,0:T(8,128)} %v_in.1) | copy-start | bytes 2073604
  4.0 0.7 %copy-start.3 = (s32[512]{0:T(512)S(1)}, s32[512]{0:T(512)}, u32[]{:S(2)}) copy-start(s32[512]{0:T(512)} %param.9) | copy-start | bytes 6148
where the time goes:
time: 68.2 us; the launch traced here: 67.5 us
  Pallas kernels  60.1 us (88%)
  local copies, waits for them, and re-layouts  6.71 us (10%)
    pallas_call x1, Pallas kernels, shards(): pl.pallas_call(functools.partial(kernel, plan), out_shape=[jax.ShapeDtype...  60.1 us
    unnamed x11, local copies, waits for them, and re-layouts  6.71 us

commit v1 on v0

v1 whole, which is shorter than its diff:
```python
import functools
import math

import jax
import jax.numpy as jnp
import numpy as np
from jax import lax
from jax.experimental import pallas as pl
from jax.experimental.pallas import tpu as pltpu
from jax.sharding import PartitionSpec as P

NLON = 7200
LAT_ROWS = 3600
KMAX = 64
STEPS = 2
COURANT = 0.1
OMEGA_RATE = 1.5

LAT_STEP = math.pi / LAT_ROWS
LON_STEP = 2.0 * math.pi / NLON
TIME_STEP = COURANT * LAT_STEP
COEFFS = 2 * KMAX + 1
TOP = 16
HALO = 4
LANES = 128
MESH = pl.DeviceIdType.MESH


def up_to(value, multiple):
    return -(-value // multiple) * multiple


class Plan:
    def __init__(self, lons, lats, rows, width, filtered):
        self.lons, self.lats, self.rows, self.width = lons, lats, rows, width
        self.filtered = filtered
        self.lanes = up_to(width + 2 * HALO, LANES)
        self.tall = rows + 2 * TOP
        self.part = rows + TOP
        self.spread = self.lanes // LANES
        one = min(80, self.part - 16)
        two = self.part - one
        wide = up_to(3 * one, LANES)
        self.batches = ((8, one, 0, wide), (8 + one, two, wide, up_to(3 * two, LANES)))
        self.cols = wide + up_to(3 * two, LANES)
        self.share = up_to(COEFFS, lons) // lons
        self.pad = up_to(self.share, 8)
        self.waves = lons * self.pad


def wave_tables(plan):
    index = np.arange(plan.lons)[:, None] * plan.share + np.arange(plan.pad)[None, :]
    real = (np.arange(plan.pad)[None, :] < plan.share) & (index < COEFFS)
    index = np.where(real, index, 0).reshape(-1)
    wave = np.where(index <= KMAX, index, index - KMAX)
    lane = np.arange(plan.lanes)
    local = np.where(lane < plan.lanes - HALO, lane, lane - plan.lanes)
    column = np.arange(plan.lons)[:, None] * plan.width + local[None, :]
    turn = (wave[None, :, None] * column[:, None, :]) % NLON * (2.0 * math.pi / NLON)
    table = np.where((index <= KMAX)[None, :, None], np.cos(turn), np.sin(turn))
    table = np.where(real.reshape(-1)[None, :, None], table, 0.0).astype(np.float32)
    high = table.astype(jnp.bfloat16)
    low = (table - high.astype(np.float32)).astype(jnp.bfloat16)
    return np.stack([high, low], axis=1)


def row_tables(plan):
    row = np.arange(plan.lats)[:, None] * plan.rows + np.arange(plan.tall)[None, :] - TOP
    angle = (row + 0.5) * LAT_STEP
    cos = np.abs(np.sin(angle))
    north = np.abs(np.sin(angle - LAT_STEP))
    south = np.abs(np.sin(angle + LAT_STEP))
    signed = np.where(row < 0, -1.0, 1.0) / cos
    sin = np.cos(angle)
    half = 0.5 / LAT_STEP
    out = np.stack(
        [0.5 / LON_STEP * signed, half * north / cos, half * south / cos, 2.0 * OMEGA_RATE * sin, sin * signed],
        axis=1,
    )
    return np.broadcast_to(out[..., None], out.shape + (LANES,)).astype(np.float32)


def stage(plan, geo, source, base, target, factor, first, stop, work=None, at=0, rows=0):
    half = 0.5 / LAT_STEP
    spread = plan.spread
    off = plan.width - (plan.lanes - LANES)

    def piece(start, size, put):
        here = pl.ds(start, size)
        lane = lax.broadcasted_iota(jnp.int32, (size, LANES), 1)
        a, gn, gs, m3, q = (geo[g, here, :] for g in range(5))
        east, west, own = [], [], []
        for f in range(3):
            tiles = [source[f, c, here, :] for c in range(spread)]
            right = [pltpu.roll(tile, 1, 1) for tile in tiles]
            left = [pltpu.roll(tile, LANES - 1, 1) for tile in tiles]
            own.append(tiles)
            west.append([jnp.where(lane == 0, right[c - 1], right[c]) for c in range(spread)])
            east.append([jnp.where(lane == LANES - 1, left[(c + 1) % spread], left[c]) for c in range(spread)])
        for c in range(spread):
            h, u, v = (own[f][c] for f in range(3))
            hw, uw, vw = (west[f][c] for f in range(3))
            he, ue, ve = (east[f][c] for f in range(3))
            hn, un, vn = (source[f, c, pl.ds(start - 1, size), :] for f in range(3))
            hs, us, vs = (source[f, c, pl.ds(start + 1, size), :] for f in range(3))
            ua = u * a
            vb = v * half
            m = m3 + u * q
            fh = (hw * uw - he * ue) * a + (hs * vs * gs - hn * vn * gn)
            fu = m * v - ua * (ue - uw) - vb * (un - us) - (he - hw) * a
            fv = -(m * u) - ua * (ve - vw) - vb * (vn - vs) - half * (hn - hs)
            for f, rate in enumerate((fh, fu, fv)):
                value = base[f, c, here, :] + factor * rate
                target[f, c, here, :] = value
                if work is not None:
                    if c == spread - 1:
                        value = jnp.where(lane < off, value, 0.0)
                    high, low = split(value)
                    to = pl.ds(pl.multiple_of(at + f * rows + put, 16), size)
                    work[0, to, c * LANES : (c + 1) * LANES] = high
                    work[1, to, c * LANES : (c + 1) * LANES] = low

    pairs = (stop - first) // 2

    @pl.loop(0, pairs)
    def _(pair):
        piece(pl.multiple_of(pair * 16 + first * 8, 8), 16, pair * 16)

    if (stop - first) % 2:
        piece(stop * 8 - 8, 8, 0)


def split(value):
    high = value.astype(jnp.bfloat16)
    return high, (value - high.astype(jnp.float32)).astype(jnp.bfloat16)


def kernel(
    plan, h_in, u_in, v_in, cut_ref, waves_hbm, rows_hbm, h_out, u_out, v_out,
    state, middle, strips, north_strips, got_strips, lines, got_lines,
    waves, geo, work, parts, got_parts, whole, coeffs, weights,
    blocks, local_sem, strip_send, strip_recv, line_send, line_recv,
    scatter_send, scatter_recv, gather_send, gather_recv,
):
    lon = lax.axis_index("lon")
    lat = lax.axis_index("lat")
    lons, lats, rows, width, lanes = plan.lons, plan.lats, plan.rows, plan.width, plan.lanes
    tall, part, half = plan.tall, plan.part, plan.lons // 2
    last = lats - 1
    end = TOP + rows
    edge = lanes - LANES
    off = width - edge

    get_waves = pltpu.make_async_copy(waves_hbm.at[lon], waves, local_sem.at[0])
    get_rows = pltpu.make_async_copy(rows_hbm.at[lat], geo, local_sem.at[1])
    get_blocks = [
        pltpu.make_async_copy(ref, blocks.at[f], local_sem.at[2 + f]) for f, ref in enumerate((h_in, u_in, v_in))
    ]
    for copy in get_blocks:
        copy.start()
    get_rows.start()
    get_waves.start()

    def around(by):
        return lax.rem(lon + by + lons, lons)

    barrier = pltpu.get_barrier_semaphore()
    for by in range(1, lons):
        pl.semaphore_signal(barrier, inc=1, device_id={"lon": around(by), "lat": lat}, device_id_type=MESH)

    @pl.when(lat > 0)
    def _():
        for by in (-1, 0, 1):
            pl.semaphore_signal(barrier, inc=1, device_id={"lon": around(by), "lat": lat - 1}, device_id_type=MESH)

    @pl.when(lat < last)
    def _():
        for by in (-1, 0, 1):
            pl.semaphore_signal(barrier, inc=1, device_id={"lon": around(by), "lat": lat + 1}, device_id_type=MESH)

    spread = plan.spread
    rim = jnp.zeros((spread, TOP, LANES), jnp.float32)
    for f in range(3):
        state[f, :, :TOP, :] = rim
        state[f, :, end:, :] = rim
        middle[f, :, :8, :] = rim[:, :8]
        middle[f, :, tall - 8 :, :] = rim[:, :8]
        state[f, spread - 1, TOP:end, :] = jnp.zeros((rows, LANES), jnp.float32)
        get_blocks[f].wait()
        for c in range(spread):
            size = min(LANES, width - c * LANES)
            state[f, c, TOP:end, :size] = blocks[f, :, c * LANES : c * LANES + size]
    for _, count, begin, size in plan.batches:
        if size > 3 * count:
            work[:, begin + 3 * count : begin + size, :] = jnp.zeros((2, size - 3 * count, lanes), jnp.bfloat16)

    blank = jnp.zeros((256 - rows, LANES), jnp.float32)
    for f in range(3):
        at = slice(HALO * f, HALO * f + HALO)
        first = jnp.concatenate([state[f, 0, TOP:end, :], blank], axis=0).T
        final = jnp.concatenate([state[f, spread - 1, TOP:end, :], blank], axis=0).T
        strips[0, at, :] = first[:HALO]
        strips[1, at, :] = final[off - HALO : off]
        for c in range(spread):
            cut = slice(c * LANES, (c + 1) * LANES)
            lines[0, at, cut] = state[f, c, TOP : TOP + HALO, :]
            lines[1, at, cut] = state[f, c, end - HALO : end, :]
    strips[:, 12:, :] = jnp.zeros((2, 4, 256), jnp.float32)
    lines[:, 12:, :] = jnp.zeros((2, 4, lanes), jnp.float32)
    north_strips[...] = strips[...]

    @pl.when(lat == 0)
    def _():
        lane = lax.broadcasted_iota(jnp.int32, (16, 256), 1)
        row = lax.broadcasted_iota(jnp.int32, (16, 256), 0)
        flip = jnp.where(row < HALO, 1.0, -1.0)
        for side in range(2):
            strip = strips[side] * flip
            mirrored = jnp.zeros((16, 256), jnp.float32)
            for i in range(HALO):
                mirrored = jnp.where(lane == rows - 1 - i, strip[:, i : i + 1], mirrored)
            north_strips[side] = mirrored
        for f in range(3):
            sign = 1.0 if f == 0 else -1.0
            for i in range(HALO):
                for c in range(spread):
                    cut = slice(c * LANES, (c + 1) * LANES)
                    lines[0, HALO * f + HALO - 1 - i, cut] = sign * state[f, c, TOP + i, :]

    @pl.when(lat == last)
    def _():
        got_strips[:, 2] = jnp.zeros((2, 16, 256), jnp.float32)
        got_lines[1] = jnp.zeros((16, lanes), jnp.float32)

    inner = jnp.logical_and(lat > 0, lat < last)
    pl.semaphore_wait(barrier, jnp.where(inner, lons + 5, lons + 2))

    def strip_copy(source, side, slot, to_lon, to_lat, number):
        return pltpu.make_async_remote_copy(
            src_ref=source.at[side], dst_ref=got_strips.at[1 - side, slot],
            send_sem=strip_send.at[number, side], recv_sem=strip_recv.at[1 - side, slot],
            device_id={"lon": to_lon, "lat": to_lat}, device_id_type=MESH,
        )

    def line_copy(which, slot, to_lon, to_lat):
        return pltpu.make_async_remote_copy(
            src_ref=lines.at[which], dst_ref=got_lines.at[slot],
            send_sem=line_send.at[which], recv_sem=line_recv.at[slot],
            device_id={"lon": to_lon, "lat": to_lat}, device_id_type=MESH,
        )

    at_pole = lat == 0
    turn = jnp.where(at_pole, half, 0)
    to_north = jnp.where(at_pole, 0, lat - 1)
    north_line = line_copy(0, jnp.where(at_pole, 0, 1), around(turn), to_north)
    south_line = line_copy(1, 0, lon, lat + 1)
    north_slot = jnp.where(at_pole, 0, 2)
    north = [
        strip_copy(north_strips, 0, north_slot, around(turn - 1), to_north, 0),
        strip_copy(north_strips, 1, north_slot, around(turn + 1), to_north, 0),
    ]
    level = [strip_copy(strips, 0, 1, around(-1), lat, 1), strip_copy(strips, 1, 1, around(1), lat, 1)]
    south = [strip_copy(strips, 0, 0, around(-1), lat + 1, 2), strip_copy(strips, 1, 0, around(1), lat + 1, 2)]
    north_line.start()

    @pl.when(lat < last)
    def _():
        south_line.start()
        for copy in south:
            copy.start()

    for copy in level + north:
        copy.start()

    for copy in level:
        copy.wait()
    for copy in [north_line] + north:
        copy.wait_send()
    for side in range(2):
        strip_copy(strips, 1 - side, 0, lon, lat, 2).wait_recv()
    line_copy(1, 0, lon, lat).wait_recv()

    @pl.when(lat < last)
    def _():
        south_line.wait_send()
        for copy in south:
            copy.wait_send()
        for side in range(2):
            strip_copy(strips, 1 - side, 2, lon, lat, 2).wait_recv()
        line_copy(1, 1, lon, lat).wait_recv()

    lane = lax.broadcasted_iota(jnp.int32, (16, 256), 1)
    sides = []
    for side in (1, 0):
        sides.append(
            jnp.where(
                lane < TOP,
                pltpu.roll(got_strips[side, 0], (TOP - rows) % 256, 1),
                jnp.where(lane < end, pltpu.roll(got_strips[side, 1], TOP, 1), pltpu.roll(got_strips[side, 2], end, 1)),
            )
        )
    sides.append(jnp.zeros((LANES - 32, 256), jnp.float32))
    halo = jnp.concatenate(sides, axis=0).T[:tall]
    lane = lax.broadcasted_iota(jnp.int32, (tall, LANES), 1)
    for f in range(3):
        for c in range(spread):
            cut = slice(c * LANES, (c + 1) * LANES)
            state[f, c, TOP - HALO : TOP, :] = got_lines[0, HALO * f : HALO * f + HALO, cut]
            state[f, c, end : end + HALO, :] = got_lines[1, HALO * f : HALO * f + HALO, cut]
        east = pltpu.roll(halo, (off - HALO * f) % LANES, 1)
        west = pltpu.roll(halo, (LANES - HALO - 16 - HALO * f) % LANES, 1)
        state[f, spread - 1] = jnp.where(
            lane >= LANES - HALO,
            west,
            jnp.where((lane >= off) & (lane < off + HALO), east, state[f, spread - 1]),
        )

    def south_rim(ref):
        @pl.when(lat == last)
        def _():
            for f in range(3):
                ref[f, :, end : end + 1, :] = ref[f, :, end - 1 : end, :]

    south_rim(state)

    count = plan.filtered
    first_row = lat * rows - 8
    limit = count - first_row
    window = pltpu.roll(cut_ref[...], lax.rem(lats * count - first_row, count), 1)[:, : plan.part]
    place = lax.broadcasted_iota(jnp.int32, (1, plan.part), 1)
    for i in range(8):
        window = jnp.where(at_pole & (place == 7 - i), cut_ref[0:1, i : i + 1], window)
    index = lon * plan.share + lax.broadcasted_iota(jnp.int32, (plan.pad, 1), 0)
    wave = jnp.where(index <= KMAX, index, index - KMAX)
    scale = jnp.where(index == 0, 1.0 / NLON, 2.0 / NLON)
    for first, count, begin, size in plan.batches:
        cut = [window[:, first - 8 : first - 8 + count]] * 3
        if size > 3 * count:
            cut.append(jnp.zeros((1, size - 3 * count), jnp.int32))
        weights[:, begin : begin + size] = jnp.where(wave <= jnp.concatenate(cut, axis=1), scale, 0.0)

    get_rows.wait()
    get_waves.wait()
    table = waves[...].reshape(2 * plan.waves, lanes)

    def advance(first, stop):
        stage(plan, geo, state, state, middle, 0.5 * TIME_STEP, first, stop)

    def share_of(ref, step, place, batch):
        _, _, begin, size = plan.batches[batch]
        return ref.at[step, place, :, begin : begin + size]

    def scatter(step, batch, by):
        return pltpu.make_async_remote_copy(
            src_ref=share_of(parts, step, around(by), batch), dst_ref=share_of(got_parts, step, by, batch),
            send_sem=scatter_send.at[step, batch, by], recv_sem=scatter_recv.at[step, batch, by],
            device_id={"lon": around(by), "lat": lat}, device_id_type=MESH,
        )

    def gather(step, batch, by, place):
        return pltpu.make_async_remote_copy(
            src_ref=share_of(whole, step, lon, batch), dst_ref=share_of(whole, step, place, batch),
            send_sem=gather_send.at[step, batch, by], recv_sem=gather_recv.at[step, batch, by],
            device_id={"lon": around(by), "lat": lat}, device_id_type=MESH,
        )

    def project(step, batch):
        first, count, begin, size = plan.batches[batch]
        stage(
            plan, geo, middle, state, state, TIME_STEP, first // 8, (first + count) // 8, work, begin, count
        )

        def against(left, value):
            return lax.dot_general(left, value, (((1,), (1,)), ((), ())), preferred_element_type=jnp.float32)

        for left in range(begin, begin + size, 256):
            width = min(256, begin + size - left)
            both = against(table, work[0, left : left + width, :])
            total = both[: plan.waves] + (both[plan.waves :] + against(waves[0], work[1, left : left + width, :]))
            parts[step, :, :, left : left + width] = total.reshape(lons, plan.pad, width)[:, : plan.share]
        for by in range(1, lons):
            scatter(step, batch, by).start()

    def reduce(step, batch):
        _, _, begin, size = plan.batches[batch]
        at = pl.ds(begin, size)
        total = parts[step, lon, :, at]
        for by in range(1, lons):
            scatter(step, batch, by).wait()
            total = total + got_parts[step, by, :, at]
        whole[step, lon, :, at] = total * weights[0 : plan.share, at]
        for by in range(1, lons):
            gather(step, batch, by, lon).start()

    def expand(step, batch):
        first, count, begin, size = plan.batches[batch]
        for by in range(1, lons):
            gather(step, batch, by, lon).wait_send()
            gather(step, batch, by, around(-by)).wait_recv()
        got = whole[step, :, :, begin : begin + size]
        if plan.pad > plan.share:
            got = jnp.concatenate([got, jnp.zeros((lons, plan.pad - plan.share, size), jnp.float32)], axis=1)
        high, low = split(got.reshape(plan.waves, size).T)
        coeffs[0:size] = high
        coeffs[size : 2 * size] = low

        @pl.loop(0, spread // 2)
        def _(chunk):
            at = pl.ds(pl.multiple_of(chunk * 256, 256), 256)
            both = jnp.dot(coeffs[0 : 2 * size], waves[0, :, at], preferred_element_type=jnp.float32)
            value = both[:size] + (
                both[size:] + jnp.dot(coeffs[0:size], waves[1, :, at], preferred_element_type=jnp.float32)
            )
            row = lax.broadcasted_iota(jnp.int32, (count, LANES), 0) + (first - 8)
            for f in range(3):
                for c in range(2):
                    to = (f, chunk * 2 + c, pl.ds(first, count))
                    new = value[f * count : (f + 1) * count, c * LANES : (c + 1) * LANES]
                    state[to] = jnp.where(row < limit, new, state[to])

    tiles = tall // 8 - 1
    seam = plan.batches[1][0] // 8
    advance(1, seam + 1)
    for step in range(STEPS):
        project(step, 0)
        advance(seam + 1, tiles)
        south_rim(middle)
        project(step, 1)
        reduce(step, 0)
        reduce(step, 1)
        expand(step, 0)
        if step < STEPS - 1:
            advance(1, seam - 1)
            expand(step, 1)
            south_rim(state)
            advance(seam - 1, seam + 1)
        else:
            expand(step, 1)

    for f, ref in enumerate((h_out, u_out, v_out)):
        for c in range(spread):
            size = min(LANES, width - c * LANES)
            ref[:, c * LANES : c * LANES + size] = state[f, c, TOP:end, :size]


def shards(plan, height, east_wind, north_wind, cutoffs):
    f32, bf16 = jnp.float32, jnp.bfloat16
    vmem = pl.BlockSpec(memory_space=pltpu.VMEM)
    hbm = pl.BlockSpec(memory_space=pl.ANY)
    lons, tall, lanes = plan.lons, plan.tall, plan.lanes
    dma = pltpu.SemaphoreType.DMA
    block = (STEPS, lons, plan.share, plan.cols)
    return pl.pallas_call(
        functools.partial(kernel, plan),
        out_shape=[jax.ShapeDtypeStruct(height.shape, f32)] * 3,
        in_specs=[hbm] * 3 + [vmem] + [hbm] * 2,
        out_specs=[vmem] * 3,
        scratch_shapes=[
            pltpu.VMEM((3, plan.spread, tall, LANES), f32),
            pltpu.VMEM((3, plan.spread, tall, LANES), f32),
            pltpu.VMEM((2, 16, 256), f32),
            pltpu.VMEM((2, 16, 256), f32),
            pltpu.VMEM((2, 3, 16, 256), f32),
            pltpu.VMEM((2, 16, lanes), f32),
            pltpu.VMEM((2, 16, lanes), f32),
            pltpu.VMEM((2, plan.waves, lanes), bf16),
            pltpu.VMEM((5, tall, LANES), f32),
            pltpu.VMEM((2, plan.cols, lanes), bf16),
            pltpu.VMEM(block, f32),
            pltpu.VMEM(block, f32),
            pltpu.VMEM(block, f32),
            pltpu.VMEM((2 * max(batch[3] for batch in plan.batches), plan.waves), bf16),
            pltpu.VMEM((plan.pad, plan.cols), f32),
            pltpu.VMEM((3,) + height.shape, f32),
            dma((5,)),
            dma((3, 2)),
            dma((2, 3)),
            dma((2,)),
            dma((2,)),
            dma((STEPS, 2, lons)),
            dma((STEPS, 2, lons)),
            dma((STEPS, 2, lons)),
            dma((STEPS, 2, lons)),
        ],
        compiler_params=pltpu.CompilerParams(
            collective_id=0, has_side_effects=True, vmem_limit_bytes=60 * 1024 * 1024
        ),
    )(
        height, east_wind, north_wind, cutoffs.reshape(1, -1),
        jnp.asarray(wave_tables(plan)), jnp.asarray(row_tables(plan)),
    )


def solution(mesh):
    placed = (P("lat", "lon"), P("lat", "lon"), P("lat", "lon"), P())

    def program(height, east_wind, north_wind, cutoffs):
        lons, lats = mesh.shape["lon"], mesh.shape["lat"]
        rows, width = height.shape[0] // lats, height.shape[1] // lons
        plan = Plan(lons, lats, rows, width, cutoffs.shape[0])
        return jax.shard_map(
            lambda *blocks: tuple(shards(plan, *blocks)),
            mesh=mesh,
            in_specs=placed,
            out_specs=(P("lat", "lon"), P("lat", "lon"), P("lat", "lon")),
            check_vma=False,
        )(height, east_wind, north_wind, cutoffs)

    return program
```

time: 68.2 us -> 58.6 us (0.86)
  Pallas kernels: 60.1 us -> 51.4 us
    pallas_call x1, Pallas kernels: 60.1 us -> 51.4 us  [shards(): pl.pallas_call(functools.partial(kernel, plan), out_shape=[jax.ShapeDtype...]
    unnamed x11 -> x3, local copies, waits for them, and re-layouts: 6.71 us -> 6.26 us
where the time goes in v1:
time: 58.6 us; the launch traced here: 58.3 us
  Pallas kernels  51.4 us (88%)
  local copies, waits for them, and re-layouts  6.26 us (11%)
  between operations  0.64 us (1%)
    pallas_call x1, Pallas kernels, shards(): pl.pallas_call(functools.partial(kernel, plan), out_shape=[jax.ShapeDtype...  51.4 us
    unnamed x3, local copies, waits for them, and re-layouts  6.26 us

profile of v1, /device:TPU:0, one launch (start us, length us, event | category | flops | bytes accessed | tf_op | source)
XLA Modules:
  0.0 58.3 jit_solution(4919176582022673063)
XLA Ops:
  0.6 51.4 %shard_map.85 = (f32[192,900]{1,0:T(8,128)}, f32[192,900]{1,0:T(8,128)}, f32[192,900]{1,0:T(8,128)}) custom-call(f32[192,900]{1,0:T(8,128)} %h_in.1, f32[192,900]{1,0:T(8,128)} %u_in.1, f32[192,900]{1,0:T(8,128)} %v_in.1, s32[1,512]{1,0:T(1,128)} %bitcast.1, bf16[8,2,192,1024]{3,2,1,0:T(8,128)(2,1)} %constant.4.clone.waves_hbm, ...), custom_call_target="tpu_custom_call" | custom-call | tf_op jit(solution)/shard_map/pallas_call | solution.py:453
  52.0 2.1 %copy.12 = f32[192,900]{1,0:T(8,128)} copy(f32[192,900]{1,0:T(8,128)} %get-tuple-element.6) | data formatting | bytes 1382400
  54.1 2.1 %copy.13 = f32[192,900]{1,0:T(8,128)} copy(f32[192,900]{1,0:T(8,128)} %get-tuple-element.7) | data formatting | bytes 1382400
  56.2 2.1 %copy.14 = f32[192,900]{1,0:T(8,128)} copy(f32[192,900]{1,0:T(8,128)} %get-tuple-element.8) | data formatting | bytes 1382400

commit v2 on v1

--- a/solution.py
+++ b/solution.py
@@ -80,27 +80,34 @@
     return np.broadcast_to(out[..., None], out.shape + (LANES,)).astype(np.float32)
 
 
-def stage(plan, geo, source, base, target, factor, first, stop, work=None, at=0, rows=0):
+def stage(plan, geo, source, base, target, factor, first, stop, work=None, at=0, rows=0, cs=None):
     half = 0.5 / LAT_STEP
     spread = plan.spread
     off = plan.width - (plan.lanes - LANES)
+    cs = range(spread) if cs is None else cs
 
     def piece(start, size, put):
         here = pl.ds(start, size)
         lane = lax.broadcasted_iota(jnp.int32, (size, LANES), 1)
         a, gn, gs, m3, q = (geo[g, here, :] for g in range(5))
-        east, west, own = [], [], []
-        for f in range(3):
-            tiles = [source[f, c, here, :] for c in range(spread)]
-            right = [pltpu.roll(tile, 1, 1) for tile in tiles]
-            left = [pltpu.roll(tile, LANES - 1, 1) for tile in tiles]
-            own.append(tiles)
-            west.append([jnp.where(lane == 0, right[c - 1], right[c]) for c in range(spread)])
-            east.append([jnp.where(lane == LANES - 1, left[(c + 1) % spread], left[c]) for c in range(spread)])
-        for c in range(spread):
-            h, u, v = (own[f][c] for f in range(3))
-            hw, uw, vw = (west[f][c] for f in range(3))
-            he, ue, ve = (east[f][c] for f in range(3))
+        kept = {}
+
+        def rolled(f, c, by):
+            c = c % spread
+            if (f, c, by) not in kept:
+                kept[f, c, by] = pltpu.roll(source[f, c, here, :], by, 1)
+            return kept[f, c, by]
+
+        def west(f, c):
+            return jnp.where(lane == 0, rolled(f, c - 1, 1), rolled(f, c, 1))
+
+        def east(f, c):
+            return jnp.where(lane == LANES - 1, rolled(f, c + 1, LANES - 1), rolled(f, c, LANES - 1))
+
+        for c in cs:
+            h, u, v = (source[f, c, here, :] for f in range(3))
+            hw, uw, vw = (west(f, c) for f in range(3))
+            he, ue, ve = (east(f, c) for f in range(3))
             hn, un, vn = (source[f, c, pl.ds(start - 1, size), :] for f in range(3))
             hs, us, vs = (source[f, c, pl.ds(start + 1, size), :] for f in range(3))
             ua = u * a
@@ -272,6 +279,16 @@
     for copy in level + north:
         copy.start()
 
+    get_rows.wait()
+    near, far = TOP // 8 + 1, end // 8 - 1
+    inside = range(1, spread - 1)
+    outside = (0, spread - 1)
+
+    def advance(first, stop, cs=None):
+        stage(plan, geo, state, state, middle, 0.5 * TIME_STEP, first, stop, cs=cs)
+
+    advance(near, far, inside)
+
     for copy in level:
         copy.wait()
     for copy in [north_line] + north:
@@ -339,12 +356,8 @@
             cut.append(jnp.zeros((1, size - 3 * count), jnp.int32))
         weights[:, begin : begin + size] = jnp.where(wave <= jnp.concatenate(cut, axis=1), scale, 0.0)
 
-    get_rows.wait()
     get_waves.wait()
     table = waves[...].reshape(2 * plan.waves, lanes)
-
-    def advance(first, stop):
-        stage(plan, geo, state, state, middle, 0.5 * TIME_STEP, first, stop)
 
     def share_of(ref, step, place, batch):
         _, _, begin, size = plan.batches[batch]
@@ -364,11 +377,14 @@
             device_id={"lon": around(by), "lat": lat}, device_id_type=MESH,
         )
 
-    def project(step, batch):
+    def finish(batch):
         first, count, begin, size = plan.batches[batch]
         stage(
             plan, geo, middle, state, state, TIME_STEP, first // 8, (first + count) // 8, work, begin, count
         )
+
+    def project(step, batch):
+        _, _, begin, size = plan.batches[batch]
 
         def against(left, value):
             return lax.dot_general(left, value, (((1,), (1,)), ((), ())), preferred_element_type=jnp.float32)
@@ -420,41 +436,78 @@
 
     tiles = tall // 8 - 1
     seam = plan.batches[1][0] // 8
-    advance(1, seam + 1)
+    outs = (h_out, u_out, v_out)
+
+    def given(f, begin, stop):
+        span = pl.ds(begin, stop - begin)
+        number = 5 + f + (3 if begin else 0)
+        return pltpu.make_async_copy(blocks.at[f, span], outs[f].at[span], local_sem.at[number])
+
+    def give(begin, stop):
+        for f in range(3):
+            for c in range(spread):
+                size = min(LANES, width - c * LANES)
+                blocks[f, begin:stop, c * LANES : c * LANES + size] = state[f, c, TOP + begin : TOP + stop, :size]
+            given(f, begin, stop).start()
+
+    advance(1, near)
+    advance(near, seam + 1, outside)
     for step in range(STEPS):
+        finish(0)
         project(step, 0)
-        advance(seam + 1, tiles)
+        if step == 0:
+            advance(seam + 1, far, outside)
+            advance(far, tiles)
+        else:
+            advance(seam + 1, tiles)
         south_rim(middle)
+        finish(1)
+        reduce(step, 0)
         project(step, 1)
-        reduce(step, 0)
+        expand(step, 0)
         reduce(step, 1)
-        expand(step, 0)
         if step < STEPS - 1:
             advance(1, seam - 1)
             expand(step, 1)
             south_rim(state)
             advance(seam - 1, seam + 1)
         else:
+            split_row = seam * 8 - TOP
+            give(0, split_row)
             expand(step, 1)
-
-    for f, ref in enumerate((h_out, u_out, v_out)):
-        for c in range(spread):
-            size = min(LANES, width - c * LANES)
-            ref[:, c * LANES : c * LANES + size] = state[f, c, TOP:end, :size]
+            give(split_row, rows)
+            for f in range(3):
+                given(f, 0, split_row).wait()
+                given(f, split_row, rows).wait()
+
+
+def hand_over(rows, *refs):
+    sources, targets, sem = refs[:3], refs[3:6], refs[6]
+    half = up_to(rows // 2, 8)
+    copies = []
+    for f in range(3):
+        for i, span in enumerate((pl.ds(0, half), pl.ds(half, rows - half))):
+            copies.append(pltpu.make_async_copy(sources[f].at[span], targets[f].at[span], sem.at[2 * f + i]))
+    for copy in copies:
+        copy.start()
+    for copy in copies:
+        copy.wait()
 
 
 def shards(plan, height, east_wind, north_wind, cutoffs):
     f32, bf16 = jnp.float32, jnp.bfloat16
     vmem = pl.BlockSpec(memory_space=pltpu.VMEM)
-    hbm = pl.BlockSpec(memory_space=pl.ANY)
+    hbm = pl.BlockSpec(memory_space=pltpu.HBM)
     lons, tall, lanes = plan.lons, plan.tall, plan.lanes
     dma = pltpu.SemaphoreType.DMA
     block = (STEPS, lons, plan.share, plan.cols)
-    return pl.pallas_call(
+    shapes = [jax.ShapeDtypeStruct(height.shape, f32)] * 3
+    params = pltpu.CompilerParams(vmem_limit_bytes=60 * 1024 * 1024)
+    final = pl.pallas_call(
         functools.partial(kernel, plan),
-        out_shape=[jax.ShapeDtypeStruct(height.shape, f32)] * 3,
+        out_shape=shapes,
         in_specs=[hbm] * 3 + [vmem] + [hbm] * 2,
-        out_specs=[vmem] * 3,
+        out_specs=[hbm] * 3,
         scratch_shapes=[
             pltpu.VMEM((3, plan.spread, tall, LANES), f32),
             pltpu.VMEM((3, plan.spread, tall, LANES), f32),
@@ -472,7 +525,7 @@
             pltpu.VMEM((2 * max(batch[3] for batch in plan.batches), plan.waves), bf16),
             pltpu.VMEM((plan.pad, plan.cols), f32),
             pltpu.VMEM((3,) + height.shape, f32),
-            dma((5,)),
+            dma((11,)),
             dma((3, 2)),
             dma((2, 3)),
             dma((2,)),
@@ -489,6 +542,14 @@
         height, east_wind, north_wind, cutoffs.reshape(1, -1),
         jnp.asarray(wave_tables(plan)), jnp.asarray(row_tables(plan)),
     )
+    return pl.pallas_call(
+        functools.partial(hand_over, height.shape[0]),
+        out_shape=shapes,
+        in_specs=[hbm] * 3,
+        out_specs=[hbm] * 3,
+        scratch_shapes=[dma((6,))],
+        compiler_params=params,
+    )(*final)
 
 
 def solution(mesh):

time: 58.6 us -> 126 us (2.15)
  Pallas kernels: 51.4 us -> 126 us
  local copies, waits for them, and re-layouts: 6.26 us -> 0 us
    pallas_call x1 -> x2, Pallas kernels: 51.4 us -> 126 us  [the longest x1 72.6 us: shards(): pl.pallas_call(functools.partial(hand_over, height.shape[0]), out_shape=s...]
    unnamed x3 -> x0, local copies, waits for them, and re-layouts: 6.26 us -> none
where the time goes in v2:
time: 126 us
  Pallas kernels  126 us (100%)
    pallas_call x1, Pallas kernels, shards(): pl.pallas_call(functools.partial(hand_over, height.shape[0]), out_shape=s...  72.6 us
    pallas_call x1, Pallas kernels, shards(): pl.pallas_call(functools.partial(kernel, plan), out_shape=shapes, in_spec...  52.9 us

profile of v2, /device:TPU:0, one launch (start us, length us, event | category | flops | bytes accessed | tf_op | source)
XLA Modules:
  0.0 126.2 jit_solution(9846013501356378508)
XLA Ops:
  0.6 52.9 %shard_map.85 = (f32[192,900]{1,0:T(8,128)}, f32[192,900]{1,0:T(8,128)}, f32[192,900]{1,0:T(8,128)}) custom-call(f32[192,900]{1,0:T(8,128)} %h_in.1, f32[192,900]{1,0:T(8,128)} %u_in.1, f32[192,900]{1,0:T(8,128)} %v_in.1, s32[1,512]{1,0:T(1,128)} %bitcast.1, bf16[8,2,192,1024]{3,2,1,0:T(8,128)(2,1)} %constant.4.clone.waves_hbm, ...), custom_call_target="tpu_custom_call" | custom-call | tf_op jit(solution)/shard_map/pallas_call | solution.py:506
  53.6 72.6 %shard_map.86 = (f32[192,900]{1,0:T(8,128)}, f32[192,900]{1,0:T(8,128)}, f32[192,900]{1,0:T(8,128)}) custom-call(f32[192,900]{1,0:T(8,128)} %get-tuple-element.6.refs_0_, f32[192,900]{1,0:T(8,128)} %get-tuple-element.7.refs_1_, f32[192,900]{1,0:T(8,128)} %get-tuple-element.8.refs_2_), custom_call_target="tpu_custom_call" | custom-call | tf_op jit(solution)/shard_map/pallas_call | solution.py:545

commit v3 on v1

--- a/solution.py
+++ b/solution.py
@@ -443,6 +443,24 @@
             ref[:, c * LANES : c * LANES + size] = state[f, c, TOP:end, :size]
 
 
+def hand_over(rows, *refs):
+    sources, targets, held, sem = refs[:3], refs[3:6], refs[6], refs[7]
+    half = up_to(rows // 2, 8)
+    reads, writes = [], []
+    for f in range(3):
+        for i, span in enumerate((pl.ds(0, half), pl.ds(half, rows - half))):
+            here = held.at[f, span]
+            reads.append(pltpu.make_async_copy(sources[f].at[span], here, sem.at[0, 2 * f + i]))
+            writes.append(pltpu.make_async_copy(here, targets[f].at[span], sem.at[1, 2 * f + i]))
+    for copy in reads:
+        copy.start()
+    for read, write in zip(reads, writes):
+        read.wait()
+        write.start()
+    for copy in writes:
+        copy.wait()
+
+
 def shards(plan, height, east_wind, north_wind, cutoffs):
     f32, bf16 = jnp.float32, jnp.bfloat16
     vmem = pl.BlockSpec(memory_space=pltpu.VMEM)
@@ -450,9 +468,10 @@
     lons, tall, lanes = plan.lons, plan.tall, plan.lanes
     dma = pltpu.SemaphoreType.DMA
     block = (STEPS, lons, plan.share, plan.cols)
-    return pl.pallas_call(
+    shapes = [jax.ShapeDtypeStruct(height.shape, f32)] * 3
+    final = pl.pallas_call(
         functools.partial(kernel, plan),
-        out_shape=[jax.ShapeDtypeStruct(height.shape, f32)] * 3,
+        out_shape=shapes,
         in_specs=[hbm] * 3 + [vmem] + [hbm] * 2,
         out_specs=[vmem] * 3,
         scratch_shapes=[
@@ -489,6 +508,14 @@
         height, east_wind, north_wind, cutoffs.reshape(1, -1),
         jnp.asarray(wave_tables(plan)), jnp.asarray(row_tables(plan)),
     )
+    return pl.pallas_call(
+        functools.partial(hand_over, height.shape[0]),
+        out_shape=shapes,
+        in_specs=[hbm] * 3,
+        out_specs=[hbm] * 3,
+        scratch_shapes=[pltpu.VMEM((3,) + height.shape, f32), dma((2, 6))],
+        compiler_params=pltpu.CompilerParams(vmem_limit_bytes=60 * 1024 * 1024),
+    )(*final)
 
 
 def solution(mesh):

time: 58.6 us -> 54.7 us (0.933)
  local copies, waits for them, and re-layouts: 6.26 us -> 0 us
  Pallas kernels: 51.4 us -> 53.9 us
    unnamed x3 -> x0, local copies, waits for them, and re-layouts: 6.26 us -> none
    pallas_call x1 -> x2, Pallas kernels: 51.4 us -> 53.9 us  [the longest x1 51.4 us: shards(): pl.pallas_call(functools.partial(kernel, plan), out_shape=shapes, in_spec...]
where the time goes in v3:
time: 54.7 us; the launch traced here: 54.5 us
  Pallas kernels  53.9 us (99%)
  between operations  0.64 us (1%)
    pallas_call x1, Pallas kernels, shards(): pl.pallas_call(functools.partial(kernel, plan), out_shape=shapes, in_spec...  51.4 us
    pallas_call x1, Pallas kernels, shards(): pl.pallas_call(functools.partial(hand_over, height.shape[0]), out_shape=s...  2.49 us

profile of v3, /device:TPU:0, one launch (start us, length us, event | category | flops | bytes accessed | tf_op | source)
XLA Modules:
  0.0 54.5 jit_solution(10317144436899234785)
XLA Ops:
  0.6 51.4 %shard_map.85 = (f32[192,900]{1,0:T(8,128)}, f32[192,900]{1,0:T(8,128)}, f32[192,900]{1,0:T(8,128)}) custom-call(f32[192,900]{1,0:T(8,128)} %h_in.1, f32[192,900]{1,0:T(8,128)} %u_in.1, f32[192,900]{1,0:T(8,128)} %v_in.1, s32[1,512]{1,0:T(1,128)} %bitcast.1, bf16[8,2,192,1024]{3,2,1,0:T(8,128)(2,1)} %constant.4.clone.waves_hbm, ...), custom_call_target="tpu_custom_call" | custom-call | tf_op jit(solution)/shard_map/pallas_call | solution.py:472
  52.0 2.5 %shard_map.86 = (f32[192,900]{1,0:T(8,128)}, f32[192,900]{1,0:T(8,128)}, f32[192,900]{1,0:T(8,128)}) custom-call(f32[192,900]{1,0:T(8,128)} %get-tuple-element.6.refs_0_, f32[192,900]{1,0:T(8,128)} %get-tuple-element.7.refs_1_, f32[192,900]{1,0:T(8,128)} %get-tuple-element.8.refs_2_), custom_call_target="tpu_custom_call" | custom-call | tf_op jit(solution)/shard_map/pallas_call | solution.py:511
